TPU v7x, 512 devices: a whole 4x8x8 slice. The times are simulated.
512 devices in a mesh: dp: 32 (over y, x_hi, core), ctx: 16 (over z, x_lo).
Axes of the slice: x: 4 (x_hi: 2, x_lo: 2; x = x_hi * 2 + x_lo), y: 8, z: 8, core: 2. Of those that a mesh axis runs over, the one named last changes fastest.
Arguments:
- queries: bfloat16 [32, 2048, 1536], P('dp', 'ctx'), may hold values from -5 to 5
- keys: bfloat16 [32, 2048, 1536], P('dp', 'ctx'), may hold values from -5 to 5
- values: bfloat16 [32, 2048, 1536], P('dp', 'ctx'), may hold values from -6 to 6
- grad_out: bfloat16 [32, 2048, 1536], P('dp', 'ctx'), may hold values from -6 to 6
- clip_tokens: int32 [32], replicated, may hold values from 896 to 1792, as said below
- text_tokens: int32 [32], replicated, may hold values from 64 to 256, as said below
- anchor_rank: int32 [32, 16, 32], P('dp', 'ctx'), may hold values from 0 to 31, each once within a row
- send_block: int32 [32, 16, 32], P('dp', 'ctx'), may hold values from 0 to 31, each once within a row
Outputs:
- attended: bfloat16 [32, 2048, 1536], P('dp', 'ctx')
- query_grad: bfloat16 [32, 2048, 1536], P('dp', 'ctx')
Inputs may be any that keep to these rules, and one draw needn't show every extreme that they name: `clip_tokens`: some clip has exactly 1792 latent tokens in every draw. `text_tokens`: some clip has exactly 256 text tokens in every draw. anchor_rank[e, c, :] is a permutation of 0 to 31. send_block[d, c, :] is a permutation of 0 to 31.
All inputs are finite; a program needn't handle non-finite values.
Results may differ from a plain program's by a relative error of at most 0.011.
Values may be sent and summed in bfloat16 or wider, within the bound.
A program may use at most 128 MiB of HBM per device.

v0:
```python
import jax
import jax.numpy as jnp
from jax import lax
from jax.sharding import PartitionSpec as P

DH = 128
TEXT = 256


def key_scores(local_q, block_k, factor):
    return jnp.einsum("qhd,khd->hqk", local_q, block_k, preferred_element_type=jnp.float32) * factor


def update_stats(stats, scores):
    row_max, row_sum = stats
    new_max = jnp.maximum(row_max, jnp.max(scores, axis=2))
    row_sum = row_sum * jnp.exp(row_max - new_max) + jnp.sum(
        jnp.exp(scores - new_max[..., None]), axis=2
    )
    return (new_max, row_sum)


def local(queries, keys, values, grad_out, clip_tokens, text_tokens, anchor_rank, send_block):
    ranks = lax.axis_size("dp")
    rows = queries.shape[1]
    width = queries.shape[2]
    heads = width // DH
    moved = rows // ranks
    outgoing = send_block[0, 0]
    incoming = anchor_rank[0, 0]

    def packed(array):
        return array[0].reshape(ranks, moved, width)[outgoing]

    def landing(landed):
        return landed[incoming].reshape(rows, heads, DH)

    arrived = (
        lax.all_to_all(packed(queries), "dp", split_axis=0, concat_axis=0, tiled=True),
        lax.all_to_all(packed(keys), "dp", split_axis=0, concat_axis=0, tiled=True),
        lax.all_to_all(packed(values), "dp", split_axis=0, concat_axis=0, tiled=True),
        lax.all_to_all(packed(grad_out), "dp", split_axis=0, concat_axis=0, tiled=True),
    )
    local_q, local_k, local_v, local_g = [landing(landed) for landed in arrived]
    rank_here = lax.axis_index("dp")
    clip_len = lax.dynamic_index_in_dim(clip_tokens, rank_here, 0, keepdims=False)
    text_len = lax.dynamic_index_in_dim(text_tokens, rank_here, 0, keepdims=False)
    total = rows * lax.axis_size("ctx")
    factor = DH ** (-0.5)
    span = min(512, total)

    def alive_keys(first, count):
        places = first + jnp.arange(count, dtype=jnp.int32)
        return (places < clip_len) | (places >= total - TEXT) & (places < total - TEXT + text_len)

    def masked(scores, first):
        alive = alive_keys(first, scores.shape[2])
        return jnp.where(alive[None, None, :], scores, -jnp.inf)

    def sweep(step_fn, carry, key_buffer, value_buffer):

        def visit(index, state):
            first = index * span
            block_k = lax.dynamic_slice_in_dim(key_buffer, first, span, 0)
            block_v = lax.dynamic_slice_in_dim(value_buffer, first, span, 0)
            return step_fn(state, first, block_k, block_v)

        return lax.fori_loop(0, total // span, visit, carry)

    start_stats = (
        jnp.full((heads, rows), -1e30, jnp.float32),
        jnp.zeros((heads, rows), jnp.float32),
    )
    empty_scores = jnp.zeros((heads, rows, total), jnp.float32)
    all_keys, all_values = (
        lax.all_gather(local_k, "ctx", axis=0, tiled=True),
        lax.all_gather(local_v, "ctx", axis=0, tiled=True),
    )

    def stat_step(carry, first, block_k, block_v):
        score_buffer, stats = carry
        scores = masked(key_scores(local_q, block_k, factor), first)
        score_buffer = lax.dynamic_update_slice_in_dim(score_buffer, scores, first, 2)
        return (score_buffer, update_stats(stats, scores))

    score_buffer, (row_max, row_sum) = sweep(
        stat_step, (empty_scores, start_stats), all_keys, all_values
    )

    def weights(first):
        scores = lax.dynamic_slice_in_dim(score_buffer, first, span, 2)
        return jnp.exp(scores - row_max[..., None]) / row_sum[..., None]

    def add_output(total_out, first, block_k, block_v):
        probs = weights(first).astype(jnp.bfloat16)
        return total_out + jnp.einsum(
            "hqk,khd->qhd", probs, block_v, preferred_element_type=jnp.float32
        )

    empty_out = jnp.zeros((rows, heads, DH), jnp.float32)
    output = sweep(add_output, empty_out, all_keys, all_values)
    drift = jnp.sum(local_g.astype(jnp.float32) * output, axis=2).T

    def add_grad(total_grad, first, block_k, block_v):
        probs = weights(first)
        slopes = jnp.einsum("qhd,khd->hqk", local_g, block_v, preferred_element_type=jnp.float32)
        mixed = (probs * (slopes - drift[..., None])).astype(jnp.bfloat16)
        return total_grad + jnp.einsum(
            "hqk,khd->qhd", mixed, block_k, preferred_element_type=jnp.float32
        )

    grads = sweep(add_grad, empty_out, all_keys, all_values)
    attended = output.astype(jnp.bfloat16).reshape(1, rows, width)
    query_grad = (grads * factor).astype(jnp.bfloat16).reshape(1, rows, width)
    return (attended, query_grad)


def solution(mesh):
    return jax.shard_map(
        local,
        mesh=mesh,
        in_specs=(
            P("dp", "ctx", None),
            P("dp", "ctx", None),
            P("dp", "ctx", None),
            P("dp", "ctx", None),
            P(),
            P(),
            P("dp", "ctx", None),
            P("dp", "ctx", None),
        ),
        out_specs=(P("dp", "ctx", None), P("dp", "ctx", None)),
        check_vma=False,
    )
```

profile of v0, /device:TPU:7, one launch (start us, length us, event | category | flops | bytes accessed | tf_op | source)
XLA Modules:
  0.0 403.4 jit_solution(10234461143514905612)
XLA Ops:
  10.6 10.5 %all-to-all-start.1 = ((bf16[32,4,1536]{2,1,0:T(4,128)(2,1)}), bf16[32,4,1536]{2,1,0:T(4,128)(2,1)S(1)}, u32[]{:S(2)}, u32[]{:S(2)}) async-start(bf16[32,4,1536]{2,1,0:T(4,128)(2,1)} %gather_fusion.2), calls=%async_computation.1 | async-start | bytes 786432 | tf_op jit(solution)/shard_map/all_to_all | solution.py:40
  21.8 13.3 %all-to-all-done.1 = bf16[32,4,1536]{2,1,0:T(4,128)(2,1)S(1)} async-done(((bf16[32,4,1536]{2,1,0:T(4,128)(2,1)}), bf16[32,4,1536]{2,1,0:T(4,128)(2,1)S(1)}, u32[]{:S(2)}, u32[]{:S(2)}) %all-to-all-start.1) | async-done | bytes 393248 | tf_op jit(solution)/shard_map/all_to_all | solution.py:40
  38.2 19.8 %all_to_all.20 = bf16[32,4,1536]{2,1,0:T(4,128)(2,1)S(1)} all-to-all(bf16[32,4,1536]{2,1,0:T(4,128)(2,1)S(1)} %gather_fusion), channel_id=1, replica_groups=mesh['dp'=32,'ctx'=16] {'dp'}, dimensions={0} | all-to-all | bytes 786432 | tf_op jit(solution)/shard_map/all_to_all | solution.py:41
  61.8 5.9 %all-to-all-start.2 = ((bf16[32,4,1536]{2,1,0:T(4,128)(2,1)}), bf16[32,4,1536]{2,1,0:T(4,128)(2,1)S(1)}, u32[]{:S(2)}, u32[]{:S(2)}) async-start(bf16[32,4,1536]{2,1,0:T(4,128)(2,1)} %gather_fusion.4), calls=%async_computation.2 | async-start | bytes 786432 | tf_op jit(solution)/shard_map/all_to_all | solution.py:39
  69.4 12.2 %all-to-all-done.2 = bf16[32,4,1536]{2,1,0:T(4,128)(2,1)S(1)} async-done(((bf16[32,4,1536]{2,1,0:T(4,128)(2,1)}), bf16[32,4,1536]{2,1,0:T(4,128)(2,1)S(1)}, u32[]{:S(2)}, u32[]{:S(2)}) %all-to-all-start.2) | async-done | bytes 393248 | tf_op jit(solution)/shard_map/all_to_all | solution.py:39
  81.7 11.8 %all-to-all-start.3 = ((bf16[32,4,1536]{2,1,0:T(4,128)(2,1)}), bf16[32,4,1536]{2,1,0:T(4,128)(2,1)S(1)}, u32[]{:S(2)}, u32[]{:S(2)}) async-start(bf16[32,4,1536]{2,1,0:T(4,128)(2,1)} %gather_fusion.6), calls=%async_computation.3 | async-start | bytes 786432 | tf_op jit(solution)/shard_map/all_to_all | solution.py:42
  96.5 10.9 %all-to-all-done.3 = bf16[32,4,1536]{2,1,0:T(4,128)(2,1)S(1)} async-done(((bf16[32,4,1536]{2,1,0:T(4,128)(2,1)}), bf16[32,4,1536]{2,1,0:T(4,128)(2,1)S(1)}, u32[]{:S(2)}, u32[]{:S(2)}) %all-to-all-start.3) | async-done | bytes 393248 | tf_op jit(solution)/shard_map/all_to_all | solution.py:42
  109.5 81.7 %all-gather.5.cloned.1.call-done = bf16[2048,12,128]{2,0,1:T(8,128)(2,1)} async-done(((bf16[128,12,128]{2,0,1:T(8,128)(2,1)}), bf16[2048,12,128]{2,0,1:T(8,128)(2,1)}) %all-gather.5.cloned.1.call-update) | async-done | bytes 6291472 | tf_op jit(solution)/shard_map/all_gather | solution.py:76
  191.2 5.7 %broadcast_in_dim.73 = f32[12,128,2048]{1,2,0:T(8,128)} broadcast(f32[]{:T(128)} %constant.149.clone.1), dimensions={} | broadcast | bytes 12582916 | tf_op jit(solution)/shard_map/broadcast_in_dim | solution.py:74
  196.9 27.0 %while.48 = (s32[]{:T(128)}, f32[12,128,2048]{1,2,0:T(8,128)}, f32[12,128]{1,0:T(8,128)S(1)}, f32[12,128]{1,0:T(8,128)}, s32[]{:T(128)}, /*index=5*/s32[]{:T(128...) while((s32[]{:T(128)}, f32[12,128,2048]{1,2,0:T(8,128)}, ...), condition=%wide.region_3.4_spmd.clone, body=%wide.region_0.3_spmd.clone.sunk | while | flops 206842368 | bytes 11536150 | solution.py:68
  200.0 3.1 fusion.50
  206.8 3.0 fusion.50
  213.6 3.0 fusion.50
  220.3 3.0 fusion.50
  223.9 112.6 %all-gather.3.cloned.1.call-done = bf16[2048,12,128]{2,0,1:T(8,128)(2,1)} async-done(((bf16[128,12,128]{2,0,1:T(8,128)(2,1)}), bf16[2048,12,128]{2,0,1:T(8,128)(2,1)}) %all-gather.3.cloned.1.call-update) | async-done | bytes 6291472 | tf_op jit(solution)/shard_map/all_gather | solution.py:77
  336.5 36.7 %while.49 = (s32[]{:T(128)}, f32[128,12,128]{0,2,1:T(8,128)}, bf16[2048,12,128]{2,0,1:T(8,128)(2,1)}, f32[12,128,2048]{1,2,0:T(8,128)}, f32[12,128]{1,0:T(8,128)...) while((s32[]{:T(128)}, f32[128,12,128]{0,2,1:T(8,128)}, ...), condition=%wide.region_5.6_spmd.clone, body=%wide.region_4.5_spmd.clone.sunk | while | flops 204079104 | bytes 18911424 | solution.py:68
  336.5 2.1 constant_dynamic-slice_fusion.2
  338.6 2.4 copy.43
  341.0 4.5 %fusion.53 = f32[128,12,128]{0,2,1:T(8,128)} fusion(f32[12,128,512]{2,1,0:T(8,128)} %copy.43, f32[12,128]{1,0:T(8,128)S(1)} %copy-done.9, f32[12,128]{1,0:T(8,128)S(1)} %get-tuple-element.873, bf16[2048,12,128]{2,0,1:T(8,128)(2,1)} %get-tuple-element.871, s32[]{:T(128)S(6)} %select_n.100, f32[128,12,128]{0,2,1:T(8,128)} %get-tuple-element.860, ...), kind=kOutput, calls=%fused_computation.30.clone.1 | convolution fusion | flops 204079104 | bytes 6303749 | tf_op jit(solution)/shard_map/while/body/eval_jaxpr/hqk,khd->qhd/dot_general | solution.py:96
  345.6 2.1 constant_dynamic-slice_fusion.2
  347.7 2.4 copy.43
  350.1 4.7 %fusion.53 = f32[128,12,128]{0,2,1:T(8,128)} fusion(f32[12,128,512]{2,1,0:T(8,128)} %copy.43, f32[12,128]{1,0:T(8,128)S(1)} %copy-done.9, f32[12,128]{1,0:T(8,128)S(1)} %get-tuple-element.873, bf16[2048,12,128]{2,0,1:T(8,128)(2,1)} %get-tuple-element.871, s32[]{:T(128)S(6)} %select_n.100, f32[128,12,128]{0,2,1:T(8,128)} %get-tuple-element.860, ...), kind=kOutput, calls=%fused_computation.30.clone.1 | convolution fusion | flops 204079104 | bytes 6303749 | tf_op jit(solution)/shard_map/while/body/eval_jaxpr/hqk,khd->qhd/dot_general | solution.py:96
  354.8 2.1 constant_dynamic-slice_fusion.2
  356.9 2.4 copy.43
  359.3 4.7 %fusion.53 = f32[128,12,128]{0,2,1:T(8,128)} fusion(f32[12,128,512]{2,1,0:T(8,128)} %copy.43, f32[12,128]{1,0:T(8,128)S(1)} %copy-done.9, f32[12,128]{1,0:T(8,128)S(1)} %get-tuple-element.873, bf16[2048,12,128]{2,0,1:T(8,128)(2,1)} %get-tuple-element.871, s32[]{:T(128)S(6)} %select_n.100, f32[128,12,128]{0,2,1:T(8,128)} %get-tuple-element.860, ...), kind=kOutput, calls=%fused_computation.30.clone.1 | convolution fusion | flops 204079104 | bytes 6303749 | tf_op jit(solution)/shard_map/while/body/eval_jaxpr/hqk,khd->qhd/dot_general | solution.py:96
  366.1 2.4 copy.43
  368.5 4.7 %fusion.53 = f32[128,12,128]{0,2,1:T(8,128)} fusion(f32[12,128,512]{2,1,0:T(8,128)} %copy.43, f32[12,128]{1,0:T(8,128)S(1)} %copy-done.9, f32[12,128]{1,0:T(8,128)S(1)} %get-tuple-element.873, bf16[2048,12,128]{2,0,1:T(8,128)(2,1)} %get-tuple-element.871, s32[]{:T(128)S(6)} %select_n.100, f32[128,12,128]{0,2,1:T(8,128)} %get-tuple-element.860, ...), kind=kOutput, calls=%fused_computation.30.clone.1 | convolution fusion | flops 204079104 | bytes 6303749 | tf_op jit(solution)/shard_map/while/body/eval_jaxpr/hqk,khd->qhd/dot_general | solution.py:96
  376.7 17.9 %while.50 = (s32[]{:T(128)}, f32[128,12,128]{0,2,1:T(8,128)S(1)}, bf16[2048,12,128]{2,0,1:T(8,128)(2,1)}, f32[12,128,2048]{1,2,0:T(8,128)}, f32[12,128]{1,0:T(8,...) while((s32[]{:T(128)}, f32[128,12,128]{0,2,1:T(8,128)S(1)}, ...), condition=%wide.region_8.9_spmd.clone, body=%wide.region_7.8_spmd.clone.sunk | while | flops 406978560 | bytes 8278196 | solution.py:68
  376.7 4.4 %fusion.57 = f32[128,12,128]{0,2,1:T(8,128)S(1)} fusion(bf16[2048,12,128]{2,0,1:T(8,128)(2,1)} %get-tuple-element.907, s32[]{:T(128)S(6)} %select_n.101, f32[12,128,2048]{1,2,0:T(8,128)} %get-tuple-element.908, bf16[128,12,128]{2,0,1:T(8,128)(2,1)S(1)} %get-tuple-element.912, f32[12,128]{1,0:T(8,128)S(1)} %get-tuple-element.913, ...), kind=kOutput, calls=%fused_computation.39.clone.1 | convolution fusion | flops 406978560 | bytes 8278016 | tf_op jit(solution)/shard_map/while/body/eval_jaxpr/hqk,khd->qhd/dot_general | solution.py:108
  381.2 4.4 %fusion.57 = f32[128,12,128]{0,2,1:T(8,128)S(1)} fusion(bf16[2048,12,128]{2,0,1:T(8,128)(2,1)} %get-tuple-element.907, s32[]{:T(128)S(6)} %select_n.101, f32[12,128,2048]{1,2,0:T(8,128)} %get-tuple-element.908, bf16[128,12,128]{2,0,1:T(8,128)(2,1)S(1)} %get-tuple-element.912, f32[12,128]{1,0:T(8,128)S(1)} %get-tuple-element.913, ...), kind=kOutput, calls=%fused_computation.39.clone.1 | convolution fusion | flops 406978560 | bytes 8278016 | tf_op jit(solution)/shard_map/while/body/eval_jaxpr/hqk,khd->qhd/dot_general | solution.py:108
  385.7 4.5 %fusion.57 = f32[128,12,128]{0,2,1:T(8,128)S(1)} fusion(bf16[2048,12,128]{2,0,1:T(8,128)(2,1)} %get-tuple-element.907, s32[]{:T(128)S(6)} %select_n.101, f32[12,128,2048]{1,2,0:T(8,128)} %get-tuple-element.908, bf16[128,12,128]{2,0,1:T(8,128)(2,1)S(1)} %get-tuple-element.912, f32[12,128]{1,0:T(8,128)S(1)} %get-tuple-element.913, ...), kind=kOutput, calls=%fused_computation.39.clone.1 | convolution fusion | flops 406978560 | bytes 8278016 | tf_op jit(solution)/shard_map/while/body/eval_jaxpr/hqk,khd->qhd/dot_general | solution.py:108
  390.1 4.4 %fusion.57 = f32[128,12,128]{0,2,1:T(8,128)S(1)} fusion(bf16[2048,12,128]{2,0,1:T(8,128)(2,1)} %get-tuple-element.907, s32[]{:T(128)S(6)} %select_n.101, f32[12,128,2048]{1,2,0:T(8,128)} %get-tuple-element.908, bf16[128,12,128]{2,0,1:T(8,128)(2,1)S(1)} %get-tuple-element.912, f32[12,128]{1,0:T(8,128)S(1)} %get-tuple-element.913, ...), kind=kOutput, calls=%fused_computation.39.clone.1 | convolution fusion | flops 406978560 | bytes 8278016 | tf_op jit(solution)/shard_map/while/body/eval_jaxpr/hqk,khd->qhd/dot_general | solution.py:108
  (114 shorter events, 39.1 us)
Async XLA Ops:
  7.2 30.0 %copy-start.4 = (bf16[1,128,1536]{2,1,0:T(8,128)(2,1)S(1)}, bf16[1,128,1536]{2,1,0:T(8,128)(2,1)}, u32[]{:S(2)}) copy-start(bf16[1,128,1536]{2,1,0:T(8,128)(2,1)} %param.16) | copy-start | bytes 1179652
  10.6 24.5 %all-to-all-start.1 = ((bf16[32,4,1536]{2,1,0:T(4,128)(2,1)}), bf16[32,4,1536]{2,1,0:T(4,128)(2,1)S(1)}, u32[]{:S(2)}, u32[]{:S(2)}) async-start(bf16[32,4,1536]{2,1,0:T(4,128)(2,1)} %gather_fusion.2), calls=%async_computation.1 | async-start | bytes 786432 | tf_op jit(solution)/shard_map/all_to_all | solution.py:40
  21.1 170.1 %all-gather.5.cloned.1.call-start = ((), (), s32[]{:S(2)}) async-start(), calls=%async_computation.5 | async-start | bytes 6684672 | tf_op jit(solution)/shard_map/all_gather | solution.py:76
  36.3 23.8 %copy-start.5 = (bf16[1,128,1536]{2,1,0:T(8,128)(2,1)S(1)}, bf16[1,128,1536]{2,1,0:T(8,128)(2,1)}, u32[]{:S(2)}) copy-start(bf16[1,128,1536]{2,1,0:T(8,128)(2,1)} %param.14) | copy-start | bytes 1179652
  37.2 299.4 %all-gather.3.cloned.1.call-start = ((), (), s32[]{:S(2)}) async-start(), calls=%async_computation.4 | async-start | bytes 6684672 | tf_op jit(solution)/shard_map/all_gather | solution.py:77
  38.2 29.5 %copy-start.6 = (bf16[1,128,1536]{2,1,0:T(8,128)(2,1)S(1)}, bf16[1,128,1536]{2,1,0:T(8,128)(2,1)}, u32[]{:S(2)}) copy-start(bf16[1,128,1536]{2,1,0:T(8,128)(2,1)} %param.17) | copy-start | bytes 1179652
  59.2 34.3 %copy-start.12 = (s32[32]{0:T(128)S(1)}, s32[32]{0:T(128)}, u32[]{:S(2)}) copy-start(s32[32]{0:T(128)} %param.19) | copy-start | bytes 388
  59.2 34.9 %copy-start.13 = (s32[32]{0:T(128)S(1)}, s32[32]{0:T(128)}, u32[]{:S(2)}) copy-start(s32[32]{0:T(128)} %param.18) | copy-start | bytes 388
  61.8 19.9 %all-to-all-start.2 = ((bf16[32,4,1536]{2,1,0:T(4,128)(2,1)}), bf16[32,4,1536]{2,1,0:T(4,128)(2,1)S(1)}, u32[]{:S(2)}, u32[]{:S(2)}) async-start(bf16[32,4,1536]{2,1,0:T(4,128)(2,1)} %gather_fusion.4), calls=%async_computation.2 | async-start | bytes 786432 | tf_op jit(solution)/shard_map/all_to_all | solution.py:39
  81.7 25.7 %all-to-all-start.3 = ((bf16[32,4,1536]{2,1,0:T(4,128)(2,1)}), bf16[32,4,1536]{2,1,0:T(4,128)(2,1)S(1)}, u32[]{:S(2)}, u32[]{:S(2)}) async-start(bf16[32,4,1536]{2,1,0:T(4,128)(2,1)} %gather_fusion.6), calls=%async_computation.3 | async-start | bytes 786432 | tf_op jit(solution)/shard_map/all_to_all | solution.py:42
  108.6 88.3 %copy-start = (bf16[128,12,128]{2,1,0:T(8,128)(2,1)}, bf16[128,12,128]{2,1,0:T(8,128)(2,1)S(1)}, u32[]{:S(2)}) copy-start(bf16[128,12,128]{2,1,0:T(8,128)(2,1)S(1)} %reshape.99) | copy-start | bytes 1179652
  197.5 0.5 copy-start.11
  200.0 3.1 copy-start.7
  203.1 0.6 copy-start.8
  204.3 0.5 copy-start.11
  206.8 3.0 copy-start.7
  209.9 0.6 copy-start.8
  211.0 0.5 copy-start.11
  213.5 3.0 copy-start.7
  216.6 0.6 copy-start.8
  217.7 0.5 copy-start.11
  220.3 3.0 copy-start.7
  223.3 0.6 copy-start.8
  338.6 2.4 copy-start.9
  347.7 2.4 copy-start.9
  356.9 2.4 copy-start.9
  366.1 2.4 copy-start.9
  373.3 3.0 copy-start.1
  373.3 3.4 copy-start.2
  373.3 3.4 copy-start.3
  373.3 3.4 copy-start.10
Sparse Core Ops, SparseCore 0:
  37.3 153.8 all-gather.4
  193.8 142.6 all-gather.2
where the time goes:
time: 406 us; the launch traced here: 403 us
  waiting for transfers between devices  231 us (57%)
  local copies, waits for them, and re-layouts  47.3 us (12%)
  matrix products  44.5 us (11%)
  starting transfers between devices  28.3 us (7%)
  blocking collectives  19.8 us (5%)
  other arithmetic  17.4 us (4%)
  between operations  14.9 us (4%)
    all_gather x1, waiting for transfers between devices, local(): lax.all_gather(local_v, 'ctx', axis=0, tiled=True)  113 us
    all_gather x1, waiting for transfers between devices, local(): lax.all_gather(local_k, 'ctx', axis=0, tiled=True)  81.7 us
    all_to_all x1, blocking collectives, local(): lax.all_to_all(packed(values), 'dp', split_axis=0, concat_axis=0, tiled=T...  19.8 us
    dot_general x4, matrix products, add_output(): jnp.einsum('hqk,khd->qhd', probs, block_v, preferred_element_type=jnp.flo...  18.7 us
    dynamic_slice x8, local copies, waits for them, and re-layouts, weights(): scores = lax.dynamic_slice_in_dim(score_buffer, first, span, 2)  18 us
    dot_general x4, matrix products, add_grad(): jnp.einsum('hqk,khd->qhd', mixed, block_k, preferred_element_type=jnp.flo...  17.8 us
    all_to_all x1, waiting for transfers between devices, local(): lax.all_to_all(packed(keys), 'dp', split_axis=0, concat_axis=0, tiled=True)  13.3 us
    all_to_all x1, waiting for transfers between devices, local(): lax.all_to_all(packed(queries), 'dp', split_axis=0, concat_axis=0, tiled=...  12.2 us
  transfers between devices with their start and end apart: 5, of which 5 were waited for; matrix products, arithmetic and copies ran while one was open for 10% of the time, Pallas kernels for 0%

commit v1 on v0

v1 whole, which is shorter than its diff:
```python
import functools

import jax
import jax.numpy as jnp
from jax import lax
from jax.experimental import pallas as pl
from jax.experimental.pallas import tpu as pltpu
from jax.sharding import PartitionSpec as P

DH = 128
TEXT = 256
MOVE = 4
PARTS = 4
LOG2E = 1.4426950408889634
MESH = pl.DeviceIdType.MESH


def one_hot(size, source):
    columns = lax.broadcasted_iota(jnp.int32, (source.shape[0], size), 1)
    return (columns == source).astype(jnp.float32).astype(jnp.bfloat16)


def looked_up(table_ref, index, count):
    lanes = lax.broadcasted_iota(jnp.int32, (index.shape[0], count), 1)
    table = jnp.broadcast_to(table_ref[0], (index.shape[0], count))
    return jnp.sum(jnp.where(lanes == index, table, 0), axis=1, keepdims=True)


def kernel(
    ranks, n_ctx, heads,
    clip_ref, text_ref, anchor_ref, send_ref, k_ref, q_ref, v_ref, g_ref,
    out_ref, grad_ref,
    packed, landed, by_head, head_rows, expos, ones_v, output, scale_row, by_head_out, returned,
    send1, recv1, send2, recv2, send3, recv3,
):
    rows = ranks * MOVE
    total = rows * n_ctx
    part_width = heads * DH // PARTS
    part_heads = heads // PARTS
    per_gap = heads // (n_ctx - heads) if n_ctx > heads else heads + n_ctx
    rank = lax.axis_index("dp")
    place = lax.axis_index("ctx")
    factor = DH ** (-0.5)

    def owner_of(head):
        return head + head // per_gap

    my_head = place - place // (per_gap + 1)
    owns = lax.rem(place, per_gap + 1) != per_gap

    barrier = pltpu.get_barrier_semaphore()

    def greet_rank(step, _):
        peer = lax.rem(rank + step, ranks)
        pl.semaphore_signal(barrier, inc=1, device_id=(peer, place), device_id_type=MESH)
        return 0

    def greet_place(step, _):
        peer = lax.rem(place + step, n_ctx)
        pl.semaphore_signal(barrier, inc=1, device_id=(rank, peer), device_id_type=MESH)
        return 0

    lax.fori_loop(1, ranks, greet_rank, 0)
    lax.fori_loop(1, n_ctx, greet_place, 0)

    spread = rows * PARTS
    line = lax.broadcasted_iota(jnp.int32, (spread, 1), 0)
    block = looked_up(send_ref, line // (MOVE * PARTS), ranks)
    to_send = one_hot(spread, lax.rem(line // MOVE, PARTS) * rows + block * MOVE + lax.rem(line, MOVE))
    slot = lax.rem(line, rows)
    origin = looked_up(anchor_ref, slot // MOVE, ranks)
    to_slot = one_hot(spread, origin * (MOVE * PARTS) + (line // rows) * MOVE + lax.rem(line, MOVE))

    def pack(which, ref):
        stacked = jnp.concatenate(
            [ref[0, :, part * part_width:(part + 1) * part_width] for part in range(PARTS)], axis=0
        )
        moved = jnp.dot(to_send, stacked, preferred_element_type=jnp.float32).astype(jnp.bfloat16)
        packed[which] = moved.reshape(ranks, MOVE * PARTS, part_width)

    def send_blocks(which):
        own = pltpu.make_async_copy(packed.at[which, rank], landed.at[which, rank], recv1.at[which])
        own.start()

        def send_to(peer):
            pltpu.make_async_remote_copy(
                src_ref=packed.at[which, peer],
                dst_ref=landed.at[which, rank],
                send_sem=send1.at[which],
                recv_sem=recv1.at[which],
                device_id=(peer, place),
                device_id_type=MESH,
            ).start()

        def both_ways(step, _):
            send_to(lax.rem(rank + step, ranks))
            send_to(lax.rem(rank + ranks - step, ranks))
            return 0

        lax.fori_loop(1, ranks // 2, both_ways, 0)
        send_to(lax.rem(rank + ranks // 2, ranks))

    def scatter_heads(which):
        pltpu.make_async_copy(landed.at[which], landed.at[which], recv1.at[which]).wait()
        arrived = landed[which].reshape(spread, part_width)
        ordered = jnp.dot(to_slot, arrived, preferred_element_type=jnp.float32).astype(jnp.bfloat16)
        for head in range(heads):
            part, column = head // part_heads, head % part_heads
            by_head[which, head] = ordered[part * rows:(part + 1) * rows, column * DH:(column + 1) * DH]

        def send_head(head, _):
            owner = owner_of(head)

            @pl.when(owner == place)
            def _():
                pltpu.make_async_copy(
                    by_head.at[which, head], head_rows.at[which, place], recv2.at[which]
                ).start()

            @pl.when(owner != place)
            def _():
                pltpu.make_async_remote_copy(
                    src_ref=by_head.at[which, head],
                    dst_ref=head_rows.at[which, place],
                    send_sem=send2.at[which],
                    recv_sem=recv2.at[which],
                    device_id=(rank, owner),
                    device_id_type=MESH,
                ).start()

            return 0

        lax.fori_loop(0, heads, send_head, 0)

    def head_arrived(which):
        pltpu.make_async_copy(head_rows.at[which], head_rows.at[which], recv2.at[which]).wait()

    def send_back(which, target, source):
        @pl.when(target == place)
        def _():
            pltpu.make_async_copy(source, returned.at[which, my_head], recv3.at[which]).start()

        @pl.when(target != place)
        def _():
            pltpu.make_async_remote_copy(
                src_ref=source,
                dst_ref=returned.at[which, my_head],
                send_sem=send3.at[which],
                recv_sem=recv3.at[which],
                device_id=(rank, target),
                device_id_type=MESH,
            ).start()

    sources = (k_ref, q_ref, v_ref, g_ref)
    pack(0, sources[0])
    pl.semaphore_wait(barrier, ranks - 1 + n_ctx - 1)
    send_blocks(0)
    for which in range(1, 4):
        pack(which, sources[which])
        send_blocks(which)
    for which in range(4):
        scatter_heads(which)

    @pl.when(owns)
    def _():
        head_arrived(0)
        head_arrived(1)
        head_arrived(2)
        ones_v[:, :DH] = head_rows[2].reshape(total, DH)
        ones_v[:, DH:] = jnp.ones((total, DH), jnp.bfloat16)
        clip_len = clip_ref[rank]
        text_len = text_ref[rank]
        spot = lax.broadcasted_iota(jnp.int32, (1, total), 1)
        alive = (spot < clip_len) | ((spot >= total - TEXT) & (spot < total - TEXT + text_len))
        bias = jnp.where(alive, 0.0, -jnp.inf).astype(jnp.float32)
        last_dims = (((1,), (1,)), ((), ()))

        def forward(step, _):
            tile = lax.rem(place + step, n_ctx)
            scores = lax.dot_general(
                head_rows[1, tile], head_rows[0].reshape(total, DH), last_dims,
                preferred_element_type=jnp.float32,
            ) + bias
            peak = jnp.max(scores, axis=1, keepdims=True)
            expo = jnp.exp2((scores - peak) * (factor * LOG2E)).astype(jnp.bfloat16)
            expos[tile] = expo
            summed = jnp.dot(expo, ones_v[...], preferred_element_type=jnp.float32)
            inverse = 1.0 / summed[:, DH:]
            result = summed[:, :DH] * inverse
            scale_row[tile] = inverse * factor
            output[tile] = result
            by_head_out[0, tile] = result.astype(jnp.bfloat16)
            send_back(0, tile, by_head_out.at[0, tile])
            return 0

        def backward(step, _):
            tile = lax.rem(place + step, n_ctx)
            cotangent = head_rows[3, tile]
            slopes = lax.dot_general(
                cotangent, head_rows[2].reshape(total, DH), last_dims,
                preferred_element_type=jnp.float32,
            )
            drift = jnp.sum(cotangent.astype(jnp.float32) * output[tile], axis=1, keepdims=True)
            mixed = (expos[tile].astype(jnp.float32) * (slopes - drift)).astype(jnp.bfloat16)
            grads = jnp.dot(mixed, head_rows[0].reshape(total, DH), preferred_element_type=jnp.float32)
            by_head_out[1, tile] = (grads * scale_row[tile]).astype(jnp.bfloat16)
            send_back(1, tile, by_head_out.at[1, tile])
            return 0

        lax.fori_loop(0, n_ctx, forward, 0)
        head_arrived(3)
        lax.fori_loop(0, n_ctx, backward, 0)

    for which, ref in ((0, out_ref), (1, grad_ref)):
        pltpu.make_async_copy(returned.at[which], returned.at[which], recv3.at[which]).wait()
        for head in range(heads):
            ref[0, :, head * DH:(head + 1) * DH] = returned[which, head]

    for which in range(4):
        sent = packed.at[which, pl.ds(0, ranks - 1)]
        pltpu.make_async_copy(sent, sent, send1.at[which]).wait()

    @pl.when(owns)
    def _():
        for which in range(4):
            sent = by_head.at[which, pl.ds(0, heads - 1)]
            pltpu.make_async_copy(sent, sent, send2.at[which]).wait()
        for which in range(2):
            sent = by_head_out.at[which, pl.ds(0, n_ctx - 1)]
            pltpu.make_async_copy(sent, sent, send3.at[which]).wait()

    @pl.when(jnp.logical_not(owns))
    def _():
        for which in range(4):
            sent = by_head.at[which]
            pltpu.make_async_copy(sent, sent, send2.at[which]).wait()


def local(ranks, n_ctx, queries, keys, values, grad_out, clip_tokens, text_tokens, anchor_rank, send_block):
    rows, width = queries.shape[1:]
    heads = width // DH
    total = rows * n_ctx
    shape = jax.ShapeDtypeStruct(queries.shape, jnp.bfloat16)
    vmem = pl.BlockSpec(memory_space=pltpu.VMEM)
    smem = pl.BlockSpec(memory_space=pltpu.SMEM)
    part_width = width // PARTS
    return pl.pallas_call(
        functools.partial(kernel, ranks, n_ctx, heads),
        out_shape=(shape, shape),
        in_specs=[smem, smem, vmem, vmem, vmem, vmem, vmem, vmem],
        out_specs=(vmem, vmem),
        scratch_shapes=[
            pltpu.VMEM((4, ranks, MOVE * PARTS, part_width), jnp.bfloat16),
            pltpu.VMEM((4, ranks, MOVE * PARTS, part_width), jnp.bfloat16),
            pltpu.VMEM((4, heads, rows, DH), jnp.bfloat16),
            pltpu.VMEM((4, n_ctx, rows, DH), jnp.bfloat16),
            pltpu.VMEM((n_ctx, rows, total), jnp.bfloat16),
            pltpu.VMEM((total, 2 * DH), jnp.bfloat16),
            pltpu.VMEM((n_ctx, rows, DH), jnp.float32),
            pltpu.VMEM((n_ctx, rows, DH), jnp.float32),
            pltpu.VMEM((2, n_ctx, rows, DH), jnp.bfloat16),
            pltpu.VMEM((2, heads, rows, DH), jnp.bfloat16),
            pltpu.SemaphoreType.DMA((4,)),
            pltpu.SemaphoreType.DMA((4,)),
            pltpu.SemaphoreType.DMA((4,)),
            pltpu.SemaphoreType.DMA((4,)),
            pltpu.SemaphoreType.DMA((2,)),
            pltpu.SemaphoreType.DMA((2,)),
        ],
        compiler_params=pltpu.CompilerParams(
            collective_id=0, has_side_effects=True, vmem_limit_bytes=48 * 1024 * 1024
        ),
        cost_estimate=pl.CostEstimate(
            flops=8 * total * total * DH, bytes_accessed=12 * rows * width, transcendentals=total * total
        ),
    )(clip_tokens, text_tokens, anchor_rank, send_block, keys, queries, values, grad_out)


def solution(mesh):
    split = P("dp", "ctx", None)
    return jax.shard_map(
        functools.partial(local, mesh.shape["dp"], mesh.shape["ctx"]),
        mesh=mesh,
        in_specs=(split, split, split, split, P(), P(), split, split),
        out_specs=(split, split),
        check_vma=False,
    )
```

time: 406 us -> 107 us (0.26)
  the two profiles are of different devices: /device:TPU:7 before, /device:TPU:2 now
where the time goes in v1:
time: 107 us
  Pallas kernels  98 us (92%)
  local copies, waits for them, and re-layouts  8.09 us (8%)
    pallas_call x1, Pallas kernels, local(): pl.pallas_call(functools.partial(kernel, ranks, n_ctx, heads), out_shape=...  98 us
    unnamed x18, local copies, waits for them, and re-layouts  8.09 us

profile of v1, /device:TPU:2, one launch (start us, length us, event | category | flops | bytes accessed | tf_op | source)
XLA Modules:
  0.0 106.8 jit_solution(13125456351631493366)
XLA Ops:
  0.6 0.0 copy-start
  0.6 1.0 copy-done
  1.6 0.0 copy-start.1
  1.6 1.0 copy-done.1
  2.6 0.0 copy-start.2
  2.6 1.0 copy-done.2
  3.6 0.0 copy-start.3
  3.6 1.0 copy-done.3
  4.6 0.0 copy-start.4
  4.6 0.7 copy-done.4
  5.3 0.0 copy-start.5
  5.3 0.7 copy-done.5
  5.9 0.0 copy-start.6
  5.9 0.7 copy-done.6
  6.6 0.0 copy-start.7
  6.6 0.7 copy-done.7
  7.2 98.0 %shard_map.95 = (bf16[1,128,1536]{2,1,0:T(8,128)(2,1)S(1)}, bf16[1,128,1536]{2,1,0:T(8,128)(2,1)S(1)}) custom-call(s32[32]{0:T(128)S(1)} %copy-done.4, s32[32]{0:T(128)S(1)} %copy-done.5, s32[1,1,32]{2,1,0:T(1,128)S(1)} %copy-done.6, s32[1,1,32]{2,1,0:T(1,128)S(1)} %copy-done.7, bf16[1,128,1536]{2,1,0:T(8,128)(2,1)S(1)} %copy-done, ...), custom_call_target="tpu_custom_call" | custom-call | flops 4294967296 | bytes 2359296 | tf_op jit(solution)/shard_map/pallas_call | solution.py:247
  105.3 0.7 copy.12
  106.0 0.7 copy.13
Async XLA Ops:
  0.6 1.0 copy-start
  1.6 1.0 copy-start.1
  2.6 1.0 copy-start.2
  3.6 1.0 copy-start.3
  4.6 0.7 copy-start.4
  5.3 0.7 copy-start.5
  5.9 0.7 copy-start.6
  6.6 0.7 copy-start.7

commit v2 on v1

v2 whole, which is shorter than its diff:
```python
import functools

import jax
import jax.numpy as jnp
from jax import lax
from jax.experimental import pallas as pl
from jax.experimental.pallas import tpu as pltpu
from jax.sharding import PartitionSpec as P

DH = 128
TEXT = 256
MOVE = 4
PARTS = 4
LOG2E = 1.4426950408889634
MESH = pl.DeviceIdType.MESH
F32 = jnp.float32
BF16 = jnp.bfloat16
LAST_DIMS = (((1,), (1,)), ((), ()))


def one_hot(size, source):
    columns = lax.broadcasted_iota(jnp.int32, (source.shape[0], size), 1)
    return (columns == source).astype(F32).astype(BF16)


def looked_up(table, index):
    count = table.shape[1]
    lanes = lax.broadcasted_iota(jnp.int32, (index.shape[0], count), 1)
    spread = jnp.broadcast_to(table, (index.shape[0], count))
    return jnp.sum(jnp.where(lanes == index, spread, 0), axis=1, keepdims=True)


def moved_rows(order, array):
    return jnp.dot(order, array, preferred_element_type=F32).astype(BF16)


def all_bytes(ref, sem):
    pltpu.make_async_copy(ref, ref, sem).wait()


def owner_of(head):
    inner = lax.rem(head, 6)
    return head // 6 * 8 + inner + jnp.where(inner >= 3, 1, 0) + jnp.where(inner >= 5, 1, 0)


def head_at(place):
    inner = lax.rem(place, 8)
    head = place // 8 * 6 + inner - jnp.where(inner > 3, 1, 0) - jnp.where(inner > 6, 1, 0)
    return head, (inner != 3) & (inner != 6)


def kernel(
    ranks, n_ctx, heads,
    clip_hbm, text_hbm, anchor_hbm, send_hbm, k_hbm, q_hbm, v_hbm, g_hbm,
    out_ref, grad_ref,
    clip_ref, text_ref, anchor_ref, send_ref, loaded,
    packed, landed, by_head, head_rows,
    columns, column_rows, to_ranks, from_ranks, query_rows,
    expos, ones_v, output, scale_row, results, returned,
    load_sem, dp_send, dp_recv, ctx_send, ctx_recv, back_send, back_recv,
):
    rows = ranks * MOVE
    total = rows * n_ctx
    part_width = heads * DH // PARTS
    part_heads = heads // PARTS
    groups = n_ctx // PARTS
    spread = rows * PARTS
    block_rows = MOVE * PARTS
    rank = lax.axis_index("dp")
    place = lax.axis_index("ctx")
    my_head, owns = head_at(place)
    factor = DH ** (-0.5)

    loads = [
        pltpu.make_async_copy(source, target, load_sem.at[index])
        for index, (source, target) in enumerate((
            (send_hbm, send_ref), (anchor_hbm, anchor_ref),
            (k_hbm, loaded.at[0]), (q_hbm, loaded.at[1]), (v_hbm, loaded.at[2]), (g_hbm, loaded.at[3]),
            (clip_hbm, clip_ref), (text_hbm, text_ref),
        ))
    ]
    for load in loads:
        load.start()

    barrier = pltpu.get_barrier_semaphore()

    def greet_rank(step, _):
        peer = lax.rem(rank + step, ranks)
        pl.semaphore_signal(barrier, inc=1, device_id=(peer, place), device_id_type=MESH)
        return 0

    def greet_place(step, _):
        peer = lax.rem(place + step, n_ctx)
        pl.semaphore_signal(barrier, inc=1, device_id=(rank, peer), device_id_type=MESH)
        return 0

    lax.fori_loop(1, ranks, greet_rank, 0)
    lax.fori_loop(1, n_ctx, greet_place, 0)

    loads[0].wait()
    loads[1].wait()
    line = lax.broadcasted_iota(jnp.int32, (spread, 1), 0)
    short = lax.broadcasted_iota(jnp.int32, (rows, 1), 0)
    inner = lax.rem(line, MOVE)
    send_table, anchor_table = send_ref[0], anchor_ref[0]
    block = looked_up(send_table, line // block_rows)
    to_send = one_hot(spread, lax.rem(line // MOVE, PARTS) * rows + block * MOVE + inner)
    origin = looked_up(anchor_table, lax.rem(line, rows) // MOVE)
    to_slot = one_hot(spread, origin * block_rows + (line // rows) * MOVE + inner)
    to_clip = one_hot(rows, looked_up(send_table, short // MOVE) * MOVE + lax.rem(short, MOVE))
    mix = one_hot(spread, lax.rem(line // MOVE, PARTS) * rows + (line // block_rows) * MOVE + inner)
    unmix = one_hot(spread, (lax.rem(line, rows) // MOVE) * block_rows + (line // rows) * MOVE + inner)
    to_output = one_hot(rows, looked_up(anchor_table, short // MOVE) * MOVE + lax.rem(short, MOVE))

    def pack_blocks(which, array):
        stacked = jnp.concatenate(
            [array[:, part * part_width:(part + 1) * part_width] for part in range(PARTS)], axis=0
        )
        packed[which] = moved_rows(to_send, stacked).reshape(ranks, block_rows, part_width)

    def pack_columns(which, array):
        ordered = moved_rows(to_clip, array)
        for head in range(heads):
            columns[which, head] = ordered[:, head * DH:(head + 1) * DH]

    def over_ranks(source, target, which):
        pltpu.make_async_copy(source.at[rank], target.at[rank], dp_recv.at[which]).start()

        def send_to(peer):
            pltpu.make_async_remote_copy(
                src_ref=source.at[peer],
                dst_ref=target.at[rank],
                send_sem=dp_send.at[which],
                recv_sem=dp_recv.at[which],
                device_id=(peer, place),
                device_id_type=MESH,
            ).start()

        def both_ways(step, _):
            send_to(lax.rem(rank + step, ranks))
            send_to(lax.rem(rank + ranks - step, ranks))
            return 0

        lax.fori_loop(1, ranks // 2, both_ways, 0)
        send_to(lax.rem(rank + ranks // 2, ranks))

    def over_heads(source, target, which):
        def send_head(step, _):
            head = lax.rem(step + place, heads)
            owner = owner_of(head)

            @pl.when(owner == place)
            def _():
                pltpu.make_async_copy(source.at[head], target.at[place], ctx_recv.at[which]).start()

            @pl.when(owner != place)
            def _():
                pltpu.make_async_remote_copy(
                    src_ref=source.at[head],
                    dst_ref=target.at[place],
                    send_sem=ctx_send.at[which],
                    recv_sem=ctx_recv.at[which],
                    device_id=(rank, owner),
                    device_id_type=MESH,
                ).start()

            return 0

        lax.fori_loop(0, heads, send_head, 0)

    def to_place(which, target):
        source = results.at[which, target]

        @pl.when(target == place)
        def _():
            pltpu.make_async_copy(source, returned.at[which, my_head], back_recv.at[which]).start()

        @pl.when(target != place)
        def _():
            pltpu.make_async_remote_copy(
                src_ref=source,
                dst_ref=returned.at[which, my_head],
                send_sem=back_send.at[which],
                recv_sem=back_recv.at[which],
                device_id=(rank, target),
                device_id_type=MESH,
            ).start()

    def scatter_blocks(which):
        all_bytes(landed.at[which], dp_recv.at[which])
        ordered = moved_rows(to_slot, landed[which].reshape(spread, part_width))
        for head in range(heads):
            part, column = head // part_heads, head % part_heads
            by_head[which, head] = ordered[part * rows:(part + 1) * rows, column * DH:(column + 1) * DH]
        over_heads(by_head.at[which], head_rows.at[which], which)

    def scatter_columns(which):
        all_bytes(column_rows.at[which], ctx_recv.at[2 + which])
        gathered = jnp.concatenate(
            [
                column_rows[which, group * PARTS:(group + 1) * PARTS].reshape(spread, DH)
                for group in range(groups)
            ],
            axis=1,
        )
        mixed = moved_rows(mix, gathered)
        for group in range(groups):
            piece = mixed[:, group * DH:(group + 1) * DH]
            to_ranks[which, :, group] = piece.reshape(ranks, block_rows, DH)
        over_ranks(to_ranks.at[which], from_ranks.at[which], 2 + which)

    def take_columns(which):
        all_bytes(from_ranks.at[which], dp_recv.at[2 + which])
        gathered = jnp.concatenate(
            [from_ranks[which, :, group].reshape(spread, DH) for group in range(groups)], axis=1
        )
        unmixed = moved_rows(unmix, gathered)
        for group in range(groups):
            query_rows[which, group] = unmixed[:, group * DH:(group + 1) * DH]

    loads[2].wait()
    pack_blocks(0, loaded[0, 0])
    pl.semaphore_wait(barrier, ranks - 1 + n_ctx - 1)
    over_ranks(packed.at[0], landed.at[0], 0)
    loads[3].wait()
    pack_columns(0, loaded[1, 0])
    over_heads(columns.at[0], column_rows.at[0], 2)
    loads[4].wait()
    pack_blocks(1, loaded[2, 0])
    over_ranks(packed.at[1], landed.at[1], 1)
    loads[5].wait()
    pack_columns(1, loaded[3, 0])
    over_heads(columns.at[1], column_rows.at[1], 3)
    loads[6].wait()
    loads[7].wait()

    scatter_blocks(0)

    @pl.when(owns)
    def _():
        scatter_columns(0)

    scatter_blocks(1)

    @pl.when(owns)
    def _():
        scatter_columns(1)
        all_bytes(head_rows.at[0], ctx_recv.at[0])
        take_columns(0)
        clip_len = clip_ref[rank]
        text_len = text_ref[rank]
        spot = lax.broadcasted_iota(jnp.int32, (1, total), 1)
        alive = (spot < clip_len) | ((spot >= total - TEXT) & (spot < total - TEXT + text_len))
        bias = jnp.where(alive, 0.0, -jnp.inf).astype(F32)

        def weigh(group, _):
            scores = lax.dot_general(
                query_rows[0, group], head_rows[0].reshape(total, DH), LAST_DIMS, preferred_element_type=F32
            ) + bias
            peak = jnp.max(scores, axis=1, keepdims=True)
            expos[group] = jnp.exp2((scores - peak) * (factor * LOG2E)).astype(BF16)
            return 0

        def forward(step, _):
            group = lax.rem(place // PARTS + step, groups)
            summed = jnp.dot(expos[group], ones_v[...], preferred_element_type=F32)
            inverse = 1.0 / summed[:, DH:]
            result = summed[:, :DH] * inverse
            scale_row[group] = inverse * factor
            output[group] = result
            results[0, pl.ds(group * PARTS, PARTS)] = result.astype(BF16).reshape(PARTS, rows, DH)
            for part in range(PARTS):
                to_place(0, group * PARTS + part)
            return 0

        def backward(step, _):
            group = lax.rem(place // PARTS + step, groups)
            cotangent = query_rows[1, group]
            slopes = lax.dot_general(
                cotangent, head_rows[1].reshape(total, DH), LAST_DIMS, preferred_element_type=F32
            )
            drift = jnp.sum(cotangent.astype(F32) * output[group], axis=1, keepdims=True)
            mixed = (expos[group].astype(F32) * (slopes - drift)).astype(BF16)
            grads = jnp.dot(mixed, head_rows[0].reshape(total, DH), preferred_element_type=F32)
            result = (grads * scale_row[group]).astype(BF16)
            results[1, pl.ds(group * PARTS, PARTS)] = result.reshape(PARTS, rows, DH)
            for part in range(PARTS):
                to_place(1, group * PARTS + part)
            return 0

        lax.fori_loop(0, groups, weigh, 0)
        all_bytes(head_rows.at[1], ctx_recv.at[1])
        ones_v[:, :DH] = head_rows[1].reshape(total, DH)
        ones_v[:, DH:] = jnp.ones((total, DH), BF16)
        lax.fori_loop(0, groups, forward, 0)
        take_columns(1)
        lax.fori_loop(0, groups, backward, 0)

    for which, ref in ((0, out_ref), (1, grad_ref)):
        all_bytes(returned.at[which], back_recv.at[which])
        together = jnp.concatenate([returned[which, head] for head in range(heads)], axis=1)
        ref[0] = moved_rows(to_output, together)

    for which in range(2):
        all_bytes(packed.at[which, pl.ds(0, ranks - 1)], dp_send.at[which])

    @pl.when(owns)
    def _():
        for which in range(2):
            all_bytes(by_head.at[which, pl.ds(0, heads - 1)], ctx_send.at[which])
            all_bytes(columns.at[which, pl.ds(0, heads - 1)], ctx_send.at[2 + which])
            all_bytes(to_ranks.at[which, pl.ds(0, ranks - 1)], dp_send.at[2 + which])
            all_bytes(results.at[which, pl.ds(0, n_ctx - 1)], back_send.at[which])

    @pl.when(jnp.logical_not(owns))
    def _():
        for which in range(2):
            all_bytes(by_head.at[which], ctx_send.at[which])
            all_bytes(columns.at[which], ctx_send.at[2 + which])


def local(ranks, n_ctx, queries, keys, values, grad_out, clip_tokens, text_tokens, anchor_rank, send_block):
    rows, width = queries.shape[1:]
    heads = width // DH
    total = rows * n_ctx
    groups = n_ctx // PARTS
    block_rows = MOVE * PARTS
    spread = rows * PARTS
    shape = jax.ShapeDtypeStruct(queries.shape, BF16)
    anywhere = pl.BlockSpec(memory_space=pl.ANY)
    vmem = pl.BlockSpec(memory_space=pltpu.VMEM)
    blocks = pltpu.VMEM((2, ranks, block_rows, width // PARTS), BF16)
    head_blocks = pltpu.VMEM((2, heads, rows, DH), BF16)
    place_blocks = pltpu.VMEM((2, n_ctx, rows, DH), BF16)
    rank_blocks = pltpu.VMEM((2, ranks, groups, block_rows, DH), BF16)
    return pl.pallas_call(
        functools.partial(kernel, ranks, n_ctx, heads),
        out_shape=(shape, shape),
        in_specs=[anywhere] * 8,
        out_specs=(vmem, vmem),
        scratch_shapes=[
            pltpu.SMEM(clip_tokens.shape, jnp.int32),
            pltpu.SMEM(text_tokens.shape, jnp.int32),
            pltpu.VMEM(anchor_rank.shape, jnp.int32),
            pltpu.VMEM(send_block.shape, jnp.int32),
            pltpu.VMEM((4,) + queries.shape, BF16),
            blocks,
            blocks,
            head_blocks,
            place_blocks,
            head_blocks,
            place_blocks,
            rank_blocks,
            rank_blocks,
            pltpu.VMEM((2, groups, spread, DH), BF16),
            pltpu.VMEM((groups, spread, total), BF16),
            pltpu.VMEM((total, 2 * DH), BF16),
            pltpu.VMEM((groups, spread, DH), F32),
            pltpu.VMEM((groups, spread, DH), F32),
            place_blocks,
            head_blocks,
            pltpu.SemaphoreType.DMA((8,)),
            pltpu.SemaphoreType.DMA((4,)),
            pltpu.SemaphoreType.DMA((4,)),
            pltpu.SemaphoreType.DMA((4,)),
            pltpu.SemaphoreType.DMA((4,)),
            pltpu.SemaphoreType.DMA((2,)),
            pltpu.SemaphoreType.DMA((2,)),
        ],
        compiler_params=pltpu.CompilerParams(
            collective_id=0, has_side_effects=True, vmem_limit_bytes=56 * 1024 * 1024
        ),
        cost_estimate=pl.CostEstimate(
            flops=8 * total * total * DH, bytes_accessed=12 * rows * width, transcendentals=total * total
        ),
    )(clip_tokens, text_tokens, anchor_rank, send_block, keys, queries, values, grad_out)


def solution(mesh):
    split = P("dp", "ctx", None)
    return jax.shard_map(
        functools.partial(local, mesh.shape["dp"], mesh.shape["ctx"]),
        mesh=mesh,
        in_specs=(split, split, split, split, P(), P(), split, split),
        out_specs=(split, split),
        check_vma=False,
    )
```

time: 107 us -> 95.4 us (0.89)
  the two profiles are of different devices: /device:TPU:2 before, /device:TPU:1 now
where the time goes in v2:
time: 95.4 us; the launch traced here: 95.2 us
  Pallas kernels  92 us (96%)
  local copies, waits for them, and re-layouts  2.57 us (3%)
    pallas_call x1, Pallas kernels, local(): pl.pallas_call(functools.partial(kernel, ranks, n_ctx, heads), out_shape=...  92 us
    unnamed x4, local copies, waits for them, and re-layouts  2.57 us

profile of v2, /device:TPU:1, one launch (start us, length us, event | category | flops | bytes accessed | tf_op | source)
XLA Modules:
  0.0 95.2 jit_solution(16532020148502044509)
XLA Ops:
  0.6 92.0 %shard_map.95 = (bf16[1,128,1536]{2,1,0:T(8,128)(2,1)}, bf16[1,128,1536]{2,1,0:T(8,128)(2,1)}) custom-call(s32[32]{0:T(128)} %clip_hbm.1, s32[32]{0:T(128)} %text_hbm.1, s32[1,1,32]{2,1,0:T(1,128)} %anchor_hbm.1, s32[1,1,32]{2,1,0:T(1,128)} %send_hbm.1, bf16[1,128,1536]{2,1,0:T(8,128)(2,1)} %k_hbm.1, bf16[1,128,1536]{2,1,0:T(8,128)(2,1)} %q_hbm.1, ...), custom_call_target="tpu_custom_call" | custom-call | flops 4294967296 | bytes 2359296 | tf_op jit(solution)/shard_map/pallas_call | solution.py:336
  92.6 0.0 copy-start
  92.6 1.8 %copy.12 = bf16[1,128,1536]{2,1,0:T(8,128)(2,1)} copy(bf16[1,128,1536]{2,1,0:T(8,128)(2,1)} %get-tuple-element.4) | data formatting | bytes 786432
  94.5 0.0 copy-done
  94.5 0.7 copy.13
Async XLA Ops:
  92.6 1.8 %copy-start = (bf16[1,128,1536]{2,1,0:T(8,128)(2,1)S(1)}, bf16[1,128,1536]{2,1,0:T(8,128)(2,1)}, u32[]{:S(2)}) copy-start(bf16[1,128,1536]{2,1,0:T(8,128)(2,1)} %get-tuple-element.5) | copy-start | bytes 1179652

commit v3 on v2

--- a/solution.py
+++ b/solution.py
@@ -12,6 +12,7 @@
 MOVE = 4
 PARTS = 4
 LOG2E = 1.4426950408889634
+KINDS = 4
 MESH = pl.DeviceIdType.MESH
 F32 = jnp.float32
 BF16 = jnp.bfloat16
@@ -38,15 +39,32 @@
     pltpu.make_async_copy(ref, ref, sem).wait()
 
 
-def owner_of(head):
+def idle_places(kind):
+    plane = 1 - kind // 2
+    core = lax.rem(kind, 2)
+    first = 2 * (plane + 2 * core)
+    second = 2 * (plane + 2 * (1 - core)) + 1
+    return jnp.minimum(first, second), jnp.maximum(first, second)
+
+
+def owner_of(kind, head):
+    low, high = idle_places(kind)
     inner = lax.rem(head, 6)
-    return head // 6 * 8 + inner + jnp.where(inner >= 3, 1, 0) + jnp.where(inner >= 5, 1, 0)
-
-
-def head_at(place):
+    inner = inner + jnp.where(inner >= low, 1, 0)
+    inner = inner + jnp.where(inner >= high, 1, 0)
+    return head // 6 * 8 + inner
+
+
+def head_at(kind, place):
+    low, high = idle_places(kind)
     inner = lax.rem(place, 8)
-    head = place // 8 * 6 + inner - jnp.where(inner > 3, 1, 0) - jnp.where(inner > 6, 1, 0)
-    return head, (inner != 3) & (inner != 6)
+    head = place // 8 * 6 + inner - jnp.where(inner > low, 1, 0) - jnp.where(inner > high, 1, 0)
+    return head, (inner != low) & (inner != high)
+
+
+def idle_kind(place):
+    plane, side = lax.rem(place // 2, 4), lax.rem(place, 2)
+    return (1 - lax.rem(plane, 2)) * 2 + lax.rem(plane // 2 + side, 2)
 
 
 def kernel(
@@ -68,7 +86,11 @@
     block_rows = MOVE * PARTS
     rank = lax.axis_index("dp")
     place = lax.axis_index("ctx")
-    my_head, owns = head_at(place)
+    kind = lax.rem(rank, KINDS)
+    my_head, owns = head_at(kind, place)
+    idle = idle_kind(place)
+    per_kind = ranks // KINDS
+    kind_rows = rows // KINDS
     factor = DH ** (-0.5)
 
     loads = [
@@ -82,6 +104,11 @@
     for load in loads:
         load.start()
 
+    for which in range(2):
+        column_rows[which, :, pl.ds(pl.multiple_of(idle * kind_rows, kind_rows), kind_rows)] = jnp.zeros(
+            (n_ctx, kind_rows, DH), BF16
+        )
+
     barrier = pltpu.get_barrier_semaphore()
 
     def greet_rank(step, _):
@@ -107,7 +134,8 @@
     to_send = one_hot(spread, lax.rem(line // MOVE, PARTS) * rows + block * MOVE + inner)
     origin = looked_up(anchor_table, lax.rem(line, rows) // MOVE)
     to_slot = one_hot(spread, origin * block_rows + (line // rows) * MOVE + inner)
-    to_clip = one_hot(rows, looked_up(send_table, short // MOVE) * MOVE + lax.rem(short, MOVE))
+    clip = lax.rem(short // MOVE, per_kind) * KINDS + short // kind_rows
+    to_clip = one_hot(rows, looked_up(send_table, clip) * MOVE + lax.rem(short, MOVE))
     mix = one_hot(spread, lax.rem(line // MOVE, PARTS) * rows + (line // block_rows) * MOVE + inner)
     unmix = one_hot(spread, (lax.rem(line, rows) // MOVE) * block_rows + (line // rows) * MOVE + inner)
     to_output = one_hot(rows, looked_up(anchor_table, short // MOVE) * MOVE + lax.rem(short, MOVE))
@@ -147,7 +175,7 @@
     def over_heads(source, target, which):
         def send_head(step, _):
             head = lax.rem(step + place, heads)
-            owner = owner_of(head)
+            owner = owner_of(kind, head)
 
             @pl.when(owner == place)
             def _():
@@ -168,6 +196,62 @@
 
         lax.fori_loop(0, heads, send_head, 0)
 
+    def columns_to_owners(which):
+        def send_head(step, _):
+            head = lax.rem(step + place, heads)
+            for target_kind in range(KINDS):
+                owner = owner_of(target_kind, head)
+                part = pl.ds(target_kind * kind_rows, kind_rows)
+                source = columns.at[which, head, part]
+                target = column_rows.at[which, place, part]
+
+                @pl.when(owner == place)
+                def _(source=source, target=target):
+                    pltpu.make_async_copy(source, target, ctx_recv.at[2 + which]).start()
+
+                @pl.when(owner != place)
+                def _(source=source, target=target, owner=owner):
+                    pltpu.make_async_remote_copy(
+                        src_ref=source,
+                        dst_ref=target,
+                        send_sem=ctx_send.at[2 + which],
+                        recv_sem=ctx_recv.at[2 + which],
+                        device_id=(rank, owner),
+                        device_id_type=MESH,
+                    ).start()
+
+            return 0
+
+        lax.fori_loop(0, heads, send_head, 0)
+
+    def columns_to_ranks(which):
+        def send_row(step, _):
+            offset = jnp.where(lax.rem(step, 2) == 1, (step + 1) // 2, per_kind - step // 2)
+            row = lax.rem(rank // KINDS + offset, per_kind)
+            for target_kind in range(KINDS):
+                peer = row * KINDS + target_kind
+                source = to_ranks.at[which, target_kind * per_kind + row]
+                target = from_ranks.at[which, rank]
+
+                @pl.when((target_kind != idle) & (peer == rank))
+                def _(source=source, target=target):
+                    pltpu.make_async_copy(source, target, dp_recv.at[2 + which]).start()
+
+                @pl.when((target_kind != idle) & (peer != rank))
+                def _(source=source, target=target, peer=peer):
+                    pltpu.make_async_remote_copy(
+                        src_ref=source,
+                        dst_ref=target,
+                        send_sem=dp_send.at[2 + which],
+                        recv_sem=dp_recv.at[2 + which],
+                        device_id=(peer, place),
+                        device_id_type=MESH,
+                    ).start()
+
+            return 0
+
+        lax.fori_loop(0, per_kind, send_row, 0)
+
     def to_place(which, target):
         source = results.at[which, target]
 
@@ -195,7 +279,7 @@
         over_heads(by_head.at[which], head_rows.at[which], which)
 
     def scatter_columns(which):
-        all_bytes(column_rows.at[which], ctx_recv.at[2 + which])
+        all_bytes(column_rows.at[which, pl.ds(0, n_ctx // KINDS * (KINDS - 1))], ctx_recv.at[2 + which])
         gathered = jnp.concatenate(
             [
                 column_rows[which, group * PARTS:(group + 1) * PARTS].reshape(spread, DH)
@@ -207,7 +291,7 @@
         for group in range(groups):
             piece = mixed[:, group * DH:(group + 1) * DH]
             to_ranks[which, :, group] = piece.reshape(ranks, block_rows, DH)
-        over_ranks(to_ranks.at[which], from_ranks.at[which], 2 + which)
+        columns_to_ranks(which)
 
     def take_columns(which):
         all_bytes(from_ranks.at[which], dp_recv.at[2 + which])
@@ -224,27 +308,23 @@
     over_ranks(packed.at[0], landed.at[0], 0)
     loads[3].wait()
     pack_columns(0, loaded[1, 0])
-    over_heads(columns.at[0], column_rows.at[0], 2)
+    columns_to_owners(0)
     loads[4].wait()
     pack_blocks(1, loaded[2, 0])
     over_ranks(packed.at[1], landed.at[1], 1)
     loads[5].wait()
     pack_columns(1, loaded[3, 0])
-    over_heads(columns.at[1], column_rows.at[1], 3)
+    columns_to_owners(1)
     loads[6].wait()
     loads[7].wait()
 
     scatter_blocks(0)
+    scatter_columns(0)
+    scatter_blocks(1)
+    scatter_columns(1)
 
     @pl.when(owns)
     def _():
-        scatter_columns(0)
-
-    scatter_blocks(1)
-
-    @pl.when(owns)
-    def _():
-        scatter_columns(1)
         all_bytes(head_rows.at[0], ctx_recv.at[0])
         take_columns(0)
         clip_len = clip_ref[rank]
@@ -303,20 +383,21 @@
 
     for which in range(2):
         all_bytes(packed.at[which, pl.ds(0, ranks - 1)], dp_send.at[which])
+        all_bytes(columns.at[which, pl.ds(0, heads - 1)], ctx_send.at[2 + which])
+        all_bytes(columns.at[which, 0, pl.ds(0, kind_rows)], ctx_send.at[2 + which])
 
     @pl.when(owns)
     def _():
         for which in range(2):
             all_bytes(by_head.at[which, pl.ds(0, heads - 1)], ctx_send.at[which])
-            all_bytes(columns.at[which, pl.ds(0, heads - 1)], ctx_send.at[2 + which])
-            all_bytes(to_ranks.at[which, pl.ds(0, ranks - 1)], dp_send.at[2 + which])
+            all_bytes(to_ranks.at[which, pl.ds(0, (KINDS - 1) * per_kind - 1)], dp_send.at[2 + which])
             all_bytes(results.at[which, pl.ds(0, n_ctx - 1)], back_send.at[which])
 
     @pl.when(jnp.logical_not(owns))
     def _():
         for which in range(2):
             all_bytes(by_head.at[which], ctx_send.at[which])
-            all_bytes(columns.at[which], ctx_send.at[2 + which])
+            all_bytes(to_ranks.at[which, pl.ds(0, (KINDS - 1) * per_kind)], dp_send.at[2 + which])
 
 
 def local(ranks, n_ctx, queries, keys, values, grad_out, clip_tokens, text_tokens, anchor_rank, send_block):
@@ -368,7 +449,7 @@
             pltpu.SemaphoreType.DMA((2,)),
         ],
         compiler_params=pltpu.CompilerParams(
-            collective_id=0, has_side_effects=True, vmem_limit_bytes=56 * 1024 * 1024
+            collective_id=0, has_side_effects=True, vmem_limit_bytes=58 * 1024 * 1024
         ),
         cost_estimate=pl.CostEstimate(
             flops=8 * total * total * DH, bytes_accessed=12 * rows * width, transcendentals=total * total

time: 95.4 us -> 83.3 us (0.87)
  Pallas kernels: 92 us -> 79.9 us
    pallas_call x1, Pallas kernels: 92 us -> 79.9 us  [local(): pl.pallas_call(functools.partial(kernel, ranks, n_ctx, heads), out_shape=...]
where the time goes in v3:
time: 83.3 us; the launch traced here: 83.1 us
  Pallas kernels  79.9 us (96%)
  local copies, waits for them, and re-layouts  2.57 us (3%)
    pallas_call x1, Pallas kernels, local(): pl.pallas_call(functools.partial(kernel, ranks, n_ctx, heads), out_shape=...  79.9 us
    unnamed x4, local copies, waits for them, and re-layouts  2.57 us

profile of v3, /device:TPU:1, one launch (start us, length us, event | category | flops | bytes accessed | tf_op | source)
XLA Modules:
  0.0 83.1 jit_solution(13728548515998259754)
XLA Ops:
  0.6 79.9 %shard_map.95 = (bf16[1,128,1536]{2,1,0:T(8,128)(2,1)}, bf16[1,128,1536]{2,1,0:T(8,128)(2,1)}) custom-call(s32[32]{0:T(128)} %clip_hbm.1, s32[32]{0:T(128)} %text_hbm.1, s32[1,1,32]{2,1,0:T(1,128)} %anchor_hbm.1, s32[1,1,32]{2,1,0:T(1,128)} %send_hbm.1, bf16[1,128,1536]{2,1,0:T(8,128)(2,1)} %k_hbm.1, bf16[1,128,1536]{2,1,0:T(8,128)(2,1)} %q_hbm.1, ...), custom_call_target="tpu_custom_call" | custom-call | flops 4294967296 | bytes 2359296 | tf_op jit(solution)/shard_map/pallas_call | solution.py:417
  80.6 0.0 copy-start
  80.6 1.8 %copy.12 = bf16[1,128,1536]{2,1,0:T(8,128)(2,1)} copy(bf16[1,128,1536]{2,1,0:T(8,128)(2,1)} %get-tuple-element.4) | data formatting | bytes 786432
  82.4 0.0 copy-done
  82.4 0.7 copy.13
Async XLA Ops:
  80.6 1.8 %copy-start = (bf16[1,128,1536]{2,1,0:T(8,128)(2,1)S(1)}, bf16[1,128,1536]{2,1,0:T(8,128)(2,1)}, u32[]{:S(2)}) copy-start(bf16[1,128,1536]{2,1,0:T(8,128)(2,1)} %get-tuple-element.5) | copy-start | bytes 1179652

commit v4 on v3

--- a/solution.py
+++ b/solution.py
@@ -70,11 +70,11 @@
 def kernel(
     ranks, n_ctx, heads,
     clip_hbm, text_hbm, anchor_hbm, send_hbm, k_hbm, q_hbm, v_hbm, g_hbm,
-    out_ref, grad_ref,
+    returned,
     clip_ref, text_ref, anchor_ref, send_ref, loaded,
     packed, landed, by_head, head_rows,
     columns, column_rows, to_ranks, from_ranks, query_rows,
-    expos, ones_v, output, scale_row, results, returned,
+    expos, ones_v, output, scale_row, results,
     load_sem, dp_send, dp_recv, ctx_send, ctx_recv, back_send, back_recv,
 ):
     rows = ranks * MOVE
@@ -104,11 +104,6 @@
     for load in loads:
         load.start()
 
-    for which in range(2):
-        column_rows[which, :, pl.ds(pl.multiple_of(idle * kind_rows, kind_rows), kind_rows)] = jnp.zeros(
-            (n_ctx, kind_rows, DH), BF16
-        )
-
     barrier = pltpu.get_barrier_semaphore()
 
     def greet_rank(step, _):
@@ -125,21 +120,12 @@
     lax.fori_loop(1, n_ctx, greet_place, 0)
 
     loads[0].wait()
-    loads[1].wait()
     line = lax.broadcasted_iota(jnp.int32, (spread, 1), 0)
     short = lax.broadcasted_iota(jnp.int32, (rows, 1), 0)
     inner = lax.rem(line, MOVE)
-    send_table, anchor_table = send_ref[0], anchor_ref[0]
+    send_table = send_ref[0]
     block = looked_up(send_table, line // block_rows)
     to_send = one_hot(spread, lax.rem(line // MOVE, PARTS) * rows + block * MOVE + inner)
-    origin = looked_up(anchor_table, lax.rem(line, rows) // MOVE)
-    to_slot = one_hot(spread, origin * block_rows + (line // rows) * MOVE + inner)
-    clip = lax.rem(short // MOVE, per_kind) * KINDS + short // kind_rows
-    to_clip = one_hot(rows, looked_up(send_table, clip) * MOVE + lax.rem(short, MOVE))
-    mix = one_hot(spread, lax.rem(line // MOVE, PARTS) * rows + (line // block_rows) * MOVE + inner)
-    unmix = one_hot(spread, (lax.rem(line, rows) // MOVE) * block_rows + (line // rows) * MOVE + inner)
-    to_output = one_hot(rows, looked_up(anchor_table, short // MOVE) * MOVE + lax.rem(short, MOVE))
-
     def pack_blocks(which, array):
         stacked = jnp.concatenate(
             [array[:, part * part_width:(part + 1) * part_width] for part in range(PARTS)], axis=0
@@ -150,6 +136,12 @@
         ordered = moved_rows(to_clip, array)
         for head in range(heads):
             columns[which, head] = ordered[:, head * DH:(head + 1) * DH]
+
+    def far_and_near(step):
+        return lax.rem(per_kind // 2 + 3 * step, per_kind)
+
+    def head_in_turn(step):
+        return lax.rem(place * heads // n_ctx + 5 * step, heads)
 
     def over_ranks(source, target, which):
         pltpu.make_async_copy(source.at[rank], target.at[rank], dp_recv.at[which]).start()
@@ -164,17 +156,22 @@
                 device_id_type=MESH,
             ).start()
 
-        def both_ways(step, _):
-            send_to(lax.rem(rank + step, ranks))
-            send_to(lax.rem(rank + ranks - step, ranks))
-            return 0
-
-        lax.fori_loop(1, ranks // 2, both_ways, 0)
-        send_to(lax.rem(rank + ranks // 2, ranks))
+        def send_row(step, _):
+            row = lax.rem(rank // KINDS + far_and_near(step), per_kind)
+            for target_kind in range(KINDS):
+                peer = row * KINDS + target_kind
+
+                @pl.when(peer != rank)
+                def _(peer=peer):
+                    send_to(peer)
+
+            return 0
+
+        lax.fori_loop(0, per_kind, send_row, 0)
 
     def over_heads(source, target, which):
         def send_head(step, _):
-            head = lax.rem(step + place, heads)
+            head = head_in_turn(step)
             owner = owner_of(kind, head)
 
             @pl.when(owner == place)
@@ -198,7 +195,7 @@
 
     def columns_to_owners(which):
         def send_head(step, _):
-            head = lax.rem(step + place, heads)
+            head = head_in_turn(step)
             for target_kind in range(KINDS):
                 owner = owner_of(target_kind, head)
                 part = pl.ds(target_kind * kind_rows, kind_rows)
@@ -226,8 +223,7 @@
 
     def columns_to_ranks(which):
         def send_row(step, _):
-            offset = jnp.where(lax.rem(step, 2) == 1, (step + 1) // 2, per_kind - step // 2)
-            row = lax.rem(rank // KINDS + offset, per_kind)
+            row = lax.rem(rank // KINDS + far_and_near(step), per_kind)
             for target_kind in range(KINDS):
                 peer = row * KINDS + target_kind
                 source = to_ranks.at[which, target_kind * per_kind + row]
@@ -306,6 +302,8 @@
     pack_blocks(0, loaded[0, 0])
     pl.semaphore_wait(barrier, ranks - 1 + n_ctx - 1)
     over_ranks(packed.at[0], landed.at[0], 0)
+    clip = lax.rem(short // MOVE, per_kind) * KINDS + short // kind_rows
+    to_clip = one_hot(rows, looked_up(send_table, clip) * MOVE + lax.rem(short, MOVE))
     loads[3].wait()
     pack_columns(0, loaded[1, 0])
     columns_to_owners(0)
@@ -317,6 +315,19 @@
     columns_to_owners(1)
     loads[6].wait()
     loads[7].wait()
+
+    for which in range(2):
+        column_rows[which, :, pl.ds(pl.multiple_of(idle * kind_rows, kind_rows), kind_rows)] = jnp.zeros(
+            (n_ctx, kind_rows, DH), BF16
+        )
+
+    loads[1].wait()
+    anchor_table = anchor_ref[0]
+    origin = looked_up(anchor_table, lax.rem(line, rows) // MOVE)
+    to_slot = one_hot(spread, origin * block_rows + (line // rows) * MOVE + inner)
+    mix = one_hot(spread, lax.rem(line // MOVE, PARTS) * rows + (line // block_rows) * MOVE + inner)
+    unmix = one_hot(spread, (lax.rem(line, rows) // MOVE) * block_rows + (line // rows) * MOVE + inner)
+
 
     scatter_blocks(0)
     scatter_columns(0)
@@ -376,10 +387,8 @@
         take_columns(1)
         lax.fori_loop(0, groups, backward, 0)
 
-    for which, ref in ((0, out_ref), (1, grad_ref)):
+    for which in range(2):
         all_bytes(returned.at[which], back_recv.at[which])
-        together = jnp.concatenate([returned[which, head] for head in range(heads)], axis=1)
-        ref[0] = moved_rows(to_output, together)
 
     for which in range(2):
         all_bytes(packed.at[which, pl.ds(0, ranks - 1)], dp_send.at[which])
@@ -398,6 +407,31 @@
         for which in range(2):
             all_bytes(by_head.at[which], ctx_send.at[which])
             all_bytes(to_ranks.at[which, pl.ds(0, (KINDS - 1) * per_kind)], dp_send.at[2 + which])
+
+
+def in_slot_order(heads, anchor_hbm, returned_hbm, out_hbm, grad_hbm, anchor_ref, returned, ordered, load_sem, store_sem):
+    rows = returned.shape[2]
+    loads = [
+        pltpu.make_async_copy(anchor_hbm, anchor_ref, load_sem.at[2]),
+        pltpu.make_async_copy(returned_hbm.at[0], returned.at[0], load_sem.at[0]),
+        pltpu.make_async_copy(returned_hbm.at[1], returned.at[1], load_sem.at[1]),
+    ]
+    stores = [
+        pltpu.make_async_copy(ordered.at[0], out_hbm, store_sem.at[0]),
+        pltpu.make_async_copy(ordered.at[1], grad_hbm, store_sem.at[1]),
+    ]
+    for load in loads:
+        load.start()
+    loads[0].wait()
+    line = lax.broadcasted_iota(jnp.int32, (rows, 1), 0)
+    to_output = one_hot(rows, looked_up(anchor_ref[0], line // MOVE) * MOVE + lax.rem(line, MOVE))
+    for which in range(2):
+        loads[1 + which].wait()
+        together = jnp.concatenate([returned[which, head] for head in range(heads)], axis=1)
+        ordered[which, 0] = moved_rows(to_output, together)
+        stores[which].start()
+    for store in stores:
+        store.wait()
 
 
 def local(ranks, n_ctx, queries, keys, values, grad_out, clip_tokens, text_tokens, anchor_rank, send_block):
@@ -407,18 +441,16 @@
     groups = n_ctx // PARTS
     block_rows = MOVE * PARTS
     spread = rows * PARTS
-    shape = jax.ShapeDtypeStruct(queries.shape, BF16)
-    anywhere = pl.BlockSpec(memory_space=pl.ANY)
-    vmem = pl.BlockSpec(memory_space=pltpu.VMEM)
+    outside = pl.BlockSpec(memory_space=pltpu.HBM)
     blocks = pltpu.VMEM((2, ranks, block_rows, width // PARTS), BF16)
     head_blocks = pltpu.VMEM((2, heads, rows, DH), BF16)
     place_blocks = pltpu.VMEM((2, n_ctx, rows, DH), BF16)
     rank_blocks = pltpu.VMEM((2, ranks, groups, block_rows, DH), BF16)
-    return pl.pallas_call(
+    returned = pl.pallas_call(
         functools.partial(kernel, ranks, n_ctx, heads),
-        out_shape=(shape, shape),
-        in_specs=[anywhere] * 8,
-        out_specs=(vmem, vmem),
+        out_shape=jax.ShapeDtypeStruct((2, heads, rows, DH), BF16),
+        in_specs=[outside] * 8,
+        out_specs=outside,
         scratch_shapes=[
             pltpu.SMEM(clip_tokens.shape, jnp.int32),
             pltpu.SMEM(text_tokens.shape, jnp.int32),
@@ -439,7 +471,6 @@
             pltpu.VMEM((groups, spread, DH), F32),
             pltpu.VMEM((groups, spread, DH), F32),
             place_blocks,
-            head_blocks,
             pltpu.SemaphoreType.DMA((8,)),
             pltpu.SemaphoreType.DMA((4,)),
             pltpu.SemaphoreType.DMA((4,)),
@@ -455,6 +486,24 @@
             flops=8 * total * total * DH, bytes_accessed=12 * rows * width, transcendentals=total * total
         ),
     )(clip_tokens, text_tokens, anchor_rank, send_block, keys, queries, values, grad_out)
+    shape = jax.ShapeDtypeStruct(queries.shape, BF16)
+    return pl.pallas_call(
+        functools.partial(in_slot_order, heads),
+        out_shape=(shape, shape),
+        in_specs=[outside, outside],
+        out_specs=(outside, outside),
+        scratch_shapes=[
+            pltpu.VMEM(anchor_rank.shape, jnp.int32),
+            pltpu.VMEM((2, heads, rows, DH), BF16),
+            pltpu.VMEM((2,) + queries.shape, BF16),
+            pltpu.SemaphoreType.DMA((3,)),
+            pltpu.SemaphoreType.DMA((2,)),
+        ],
+        compiler_params=pltpu.CompilerParams(vmem_limit_bytes=58 * 1024 * 1024),
+        cost_estimate=pl.CostEstimate(
+            flops=4 * rows * rows * width, bytes_accessed=8 * rows * width, transcendentals=0
+        ),
+    )(anchor_rank, returned)
 
 
 def solution(mesh):

time: 83.3 us -> 81.1 us (0.974)
  the two profiles are of different devices: /device:TPU:1 before, /device:TPU:7 now
where the time goes in v4:
time: 81.1 us; the launch traced here: 79.8 us
  Pallas kernels  79.1 us (98%)
    pallas_call x1, Pallas kernels, local(): pl.pallas_call(functools.partial(kernel, ranks, n_ctx, heads), out_shape=...  76.8 us
    pallas_call x1, Pallas kernels, local(): pl.pallas_call(functools.partial(in_slot_order, heads), out_shape=(shape,...  2.31 us

profile of v4, /device:TPU:7, one launch (start us, length us, event | category | flops | bytes accessed | tf_op | source)
XLA Modules:
  0.0 79.8 jit_solution(5492472643664700842)
XLA Ops:
  0.6 76.8 %shard_map.95.returned_hbm = bf16[2,12,128,128]{3,2,1,0:T(8,128)(2,1)} custom-call(s32[32]{0:T(128)} %clip_hbm.1, s32[32]{0:T(128)} %text_hbm.1, s32[1,1,32]{2,1,0:T(1,128)} %anchor_hbm.3, s32[1,1,32]{2,1,0:T(1,128)} %send_hbm.1, bf16[1,128,1536]{2,1,0:T(8,128)(2,1)} %k_hbm.1, bf16[1,128,1536]{2,1,0:T(8,128)(2,1)} %q_hbm.1, bf16[1,128,1536]{2,1,0:T(8,128)(2,1)} %v_hbm.1, ...), custom_call_target="tpu_custom_call" | custom-call | flops 4294967296 | bytes 2359296 | tf_op jit(solution)/shard_map/pallas_call | solution.py:449
  77.5 2.3 %shard_map.96 = (bf16[1,128,1536]{2,1,0:T(8,128)(2,1)}, bf16[1,128,1536]{2,1,0:T(8,128)(2,1)}) custom-call(s32[1,1,32]{2,1,0:T(1,128)} %anchor_hbm.3, bf16[2,12,128,128]{3,2,1,0:T(8,128)(2,1)} %shard_map.95.returned_hbm), custom_call_target="tpu_custom_call" | custom-call | flops 100663296 | bytes 1572864 | tf_op jit(solution)/shard_map/pallas_call | solution.py:490

commit v5 on v4

--- a/solution.py
+++ b/solution.py
@@ -101,9 +101,6 @@
             (clip_hbm, clip_ref), (text_hbm, text_ref),
         ))
     ]
-    for load in loads:
-        load.start()
-
     barrier = pltpu.get_barrier_semaphore()
 
     def greet_rank(step, _):
@@ -116,16 +113,19 @@
         pl.semaphore_signal(barrier, inc=1, device_id=(rank, peer), device_id_type=MESH)
         return 0
 
-    lax.fori_loop(1, ranks, greet_rank, 0)
-    lax.fori_loop(1, n_ctx, greet_place, 0)
+    for index in (0, 3, 2, 5, 4, 1, 6, 7):
+        loads[index].start()
+    for step in range(1, ranks):
+        greet_rank(step, 0)
+    for step in range(1, n_ctx):
+        greet_place(step, 0)
 
     loads[0].wait()
     line = lax.broadcasted_iota(jnp.int32, (spread, 1), 0)
     short = lax.broadcasted_iota(jnp.int32, (rows, 1), 0)
     inner = lax.rem(line, MOVE)
     send_table = send_ref[0]
-    block = looked_up(send_table, line // block_rows)
-    to_send = one_hot(spread, lax.rem(line // MOVE, PARTS) * rows + block * MOVE + inner)
+
     def pack_blocks(which, array):
         stacked = jnp.concatenate(
             [array[:, part * part_width:(part + 1) * part_width] for part in range(PARTS)], axis=0
@@ -298,21 +298,23 @@
         for group in range(groups):
             query_rows[which, group] = unmixed[:, group * DH:(group + 1) * DH]
 
-    loads[2].wait()
-    pack_blocks(0, loaded[0, 0])
-    pl.semaphore_wait(barrier, ranks - 1 + n_ctx - 1)
-    over_ranks(packed.at[0], landed.at[0], 0)
     clip = lax.rem(short // MOVE, per_kind) * KINDS + short // kind_rows
     to_clip = one_hot(rows, looked_up(send_table, clip) * MOVE + lax.rem(short, MOVE))
     loads[3].wait()
     pack_columns(0, loaded[1, 0])
+    pl.semaphore_wait(barrier, ranks - 1 + n_ctx - 1)
     columns_to_owners(0)
+    block = looked_up(send_table, line // block_rows)
+    to_send = one_hot(spread, lax.rem(line // MOVE, PARTS) * rows + block * MOVE + inner)
+    loads[2].wait()
+    pack_blocks(0, loaded[0, 0])
+    over_ranks(packed.at[0], landed.at[0], 0)
+    loads[5].wait()
+    pack_columns(1, loaded[3, 0])
+    columns_to_owners(1)
     loads[4].wait()
     pack_blocks(1, loaded[2, 0])
     over_ranks(packed.at[1], landed.at[1], 1)
-    loads[5].wait()
-    pack_columns(1, loaded[3, 0])
-    columns_to_owners(1)
     loads[6].wait()
     loads[7].wait()
 

time: 81.1 us -> 80.3 us (level); the launches traced: 79.8 us -> 80.2 us
  no operation moved by 1% of the time
where the time goes in v5:
time: 80.3 us; the launch traced here: 80.2 us
  Pallas kernels  79.5 us (99%)
    pallas_call x1, Pallas kernels, local(): pl.pallas_call(functools.partial(kernel, ranks, n_ctx, heads), out_shape=...  77.2 us
    pallas_call x1, Pallas kernels, local(): pl.pallas_call(functools.partial(in_slot_order, heads), out_shape=(shape,...  2.31 us

profile of v5, /device:TPU:7, one launch (start us, length us, event | category | flops | bytes accessed | tf_op | source)
XLA Modules:
  0.0 80.2 jit_solution(18392498860281918966)
XLA Ops:
  0.6 77.2 %shard_map.95.returned_hbm = bf16[2,12,128,128]{3,2,1,0:T(8,128)(2,1)} custom-call(s32[32]{0:T(128)} %clip_hbm.1, s32[32]{0:T(128)} %text_hbm.1, s32[1,1,32]{2,1,0:T(1,128)} %anchor_hbm.3, s32[1,1,32]{2,1,0:T(1,128)} %send_hbm.1, bf16[1,128,1536]{2,1,0:T(8,128)(2,1)} %k_hbm.1, bf16[1,128,1536]{2,1,0:T(8,128)(2,1)} %q_hbm.1, bf16[1,128,1536]{2,1,0:T(8,128)(2,1)} %v_hbm.1, ...), custom_call_target="tpu_custom_call" | custom-call | flops 4294967296 | bytes 2359296 | tf_op jit(solution)/shard_map/pallas_call | solution.py:451
  77.9 2.3 %shard_map.96 = (bf16[1,128,1536]{2,1,0:T(8,128)(2,1)}, bf16[1,128,1536]{2,1,0:T(8,128)(2,1)}) custom-call(s32[1,1,32]{2,1,0:T(1,128)} %anchor_hbm.3, bf16[2,12,128,128]{3,2,1,0:T(8,128)(2,1)} %shard_map.95.returned_hbm), custom_call_target="tpu_custom_call" | custom-call | flops 100663296 | bytes 1572864 | tf_op jit(solution)/shard_map/pallas_call | solution.py:492

commit v6 on v5

--- a/solution.py
+++ b/solution.py
@@ -413,25 +413,30 @@
 
 def in_slot_order(heads, anchor_hbm, returned_hbm, out_hbm, grad_hbm, anchor_ref, returned, ordered, load_sem, store_sem):
     rows = returned.shape[2]
-    loads = [
-        pltpu.make_async_copy(anchor_hbm, anchor_ref, load_sem.at[2]),
-        pltpu.make_async_copy(returned_hbm.at[0], returned.at[0], load_sem.at[0]),
-        pltpu.make_async_copy(returned_hbm.at[1], returned.at[1], load_sem.at[1]),
-    ]
-    stores = [
-        pltpu.make_async_copy(ordered.at[0], out_hbm, store_sem.at[0]),
-        pltpu.make_async_copy(ordered.at[1], grad_hbm, store_sem.at[1]),
-    ]
-    for load in loads:
-        load.start()
-    loads[0].wait()
+    half = heads // 2
+    pieces = [(which, first) for which in range(2) for first in (0, half)]
+    anchor_load = pltpu.make_async_copy(anchor_hbm, anchor_ref, load_sem.at[4])
+    anchor_load.start()
+    loads, stores = [], []
+    for index, (which, first) in enumerate(pieces):
+        some = pl.ds(first, half)
+        columns = pl.ds(first * DH, half * DH)
+        target = (out_hbm, grad_hbm)[which]
+        loads.append(
+            pltpu.make_async_copy(returned_hbm.at[which, some], returned.at[which, some], load_sem.at[index])
+        )
+        stores.append(
+            pltpu.make_async_copy(ordered.at[which, :, :, columns], target.at[:, :, columns], store_sem.at[index])
+        )
+        loads[-1].start()
+    anchor_load.wait()
     line = lax.broadcasted_iota(jnp.int32, (rows, 1), 0)
     to_output = one_hot(rows, looked_up(anchor_ref[0], line // MOVE) * MOVE + lax.rem(line, MOVE))
-    for which in range(2):
-        loads[1 + which].wait()
-        together = jnp.concatenate([returned[which, head] for head in range(heads)], axis=1)
-        ordered[which, 0] = moved_rows(to_output, together)
-        stores[which].start()
+    for index, (which, first) in enumerate(pieces):
+        loads[index].wait()
+        together = jnp.concatenate([returned[which, first + head] for head in range(half)], axis=1)
+        ordered[which, 0, :, first * DH:(first + half) * DH] = moved_rows(to_output, together)
+        stores[index].start()
     for store in stores:
         store.wait()
 
@@ -498,8 +503,8 @@
             pltpu.VMEM(anchor_rank.shape, jnp.int32),
             pltpu.VMEM((2, heads, rows, DH), BF16),
             pltpu.VMEM((2,) + queries.shape, BF16),
-            pltpu.SemaphoreType.DMA((3,)),
-            pltpu.SemaphoreType.DMA((2,)),
+            pltpu.SemaphoreType.DMA((5,)),
+            pltpu.SemaphoreType.DMA((4,)),
         ],
         compiler_params=pltpu.CompilerParams(vmem_limit_bytes=58 * 1024 * 1024),
         cost_estimate=pl.CostEstimate(

time: 80.3 us -> 80.6 us (level)
  no operation moved by 1% of the time
where the time goes in v6:
time: 80.6 us; the launch traced here: 80.4 us
  Pallas kernels  79.8 us (99%)
    pallas_call x1, Pallas kernels, local(): pl.pallas_call(functools.partial(kernel, ranks, n_ctx, heads), out_shape=...  77.2 us
    pallas_call x1, Pallas kernels, local(): pl.pallas_call(functools.partial(in_slot_order, heads), out_shape=(shape,...  2.54 us

profile of v6, /device:TPU:7, one launch (start us, length us, event | category | flops | bytes accessed | tf_op | source)
XLA Modules:
  0.0 80.4 jit_solution(10131337181650415989)
XLA Ops:
  0.6 77.2 %shard_map.95.returned_hbm = bf16[2,12,128,128]{3,2,1,0:T(8,128)(2,1)} custom-call(s32[32]{0:T(128)} %clip_hbm.1, s32[32]{0:T(128)} %text_hbm.1, s32[1,1,32]{2,1,0:T(1,128)} %anchor_hbm.3, s32[1,1,32]{2,1,0:T(1,128)} %send_hbm.1, bf16[1,128,1536]{2,1,0:T(8,128)(2,1)} %k_hbm.1, bf16[1,128,1536]{2,1,0:T(8,128)(2,1)} %q_hbm.1, bf16[1,128,1536]{2,1,0:T(8,128)(2,1)} %v_hbm.1, ...), custom_call_target="tpu_custom_call" | custom-call | flops 4294967296 | bytes 2359296 | tf_op jit(solution)/shard_map/pallas_call | solution.py:456
  77.9 2.5 %shard_map.96 = (bf16[1,128,1536]{2,1,0:T(8,128)(2,1)}, bf16[1,128,1536]{2,1,0:T(8,128)(2,1)}) custom-call(s32[1,1,32]{2,1,0:T(1,128)} %anchor_hbm.3, bf16[2,12,128,128]{3,2,1,0:T(8,128)(2,1)} %shard_map.95.returned_hbm), custom_call_target="tpu_custom_call" | custom-call | flops 100663296 | bytes 1572864 | tf_op jit(solution)/shard_map/pallas_call | solution.py:497
